TPU v7x, 768 devices: a whole 4x8x12 slice. The times are simulated.
768 devices in a mesh: node: 16 (over x, z_hi), local: 48 (over z_lo, y, core).
Axes of the slice: x: 4, y: 8, z: 12 (z_hi: 4, z_lo: 3; z = z_hi * 3 + z_lo), core: 2. Of those that a mesh axis runs over, the one named last changes fastest.
Arguments:
- acts: bfloat16 [196608, 6144], P(('node', 'local')), may hold values from -24 to 24
- key_cot: bfloat16 [196608, 512], P(('node', 'local')), may hold values from -0.013671875 to 0.013671875
- value_cot: bfloat16 [196608, 512], P(('node', 'local')), may hold values from -0.013671875 to 0.013671875
Outputs:
- kv_grad: float32 [6144, 1024], P(('node', 'local'))
All inputs are finite; a program needn't handle non-finite values.
Results may differ from a plain program's by a relative error of at most 0.01.
Values may be sent and summed in bfloat16 or wider, within the bound.
A program may use at most 64 MiB of HBM per device.

v0:
```python
import jax
import jax.numpy as jnp
from jax import lax
from jax.sharding import PartitionSpec as P


def local_partial(acts, cotan, n_node, n_local):
    piece = lax.dot_general(
        acts, cotan, (((0,), (0,)), ((), ())), preferred_element_type=jnp.float32
    )
    slab = acts.shape[1] // (n_node * n_local)
    return piece.astype(jnp.bfloat16).reshape(n_node, n_local, slab, cotan.shape[1])


def fold_group(received):
    return jnp.sum(received.astype(jnp.float32), axis=1).astype(jnp.bfloat16)


def shards(acts, key_cot, value_cot):
    n_node = lax.axis_size("node")
    n_local = lax.axis_size("local")
    cotan = jnp.concatenate([key_cot, value_cot], axis=1)
    parts = local_partial(acts, cotan, n_node, n_local)
    received = lax.all_to_all(parts, "local", split_axis=1, concat_axis=1, tiled=True)
    grouped = fold_group(received)
    owned = lax.all_to_all(grouped, "node", split_axis=0, concat_axis=0, tiled=True)
    result = jnp.sum(owned.astype(jnp.float32), axis=0)
    return result


def solution(mesh):
    placed = (P(("node", "local"), None), P(("node", "local"), None), P(("node", "local"), None))
    return jax.shard_map(
        shards, mesh=mesh, in_specs=placed, out_specs=P(("node", "local"), None), check_vma=False
    )
```

profile of v0, /device:TPU:1, one launch (start us, length us, event | category | flops | bytes accessed | tf_op | source)
XLA Modules:
  0.0 378.4 jit_solution(18152911839274280619)
XLA Ops:
  0.0 0.0 copy-start
  0.0 1.9 copy-done
  1.9 7.4 %convert_bitcast_fusion = bf16[6144,1024]{0,1:T(8,128)(2,1)} fusion(bf16[256,6144]{1,0:T(8,128)(2,1)S(1)} %copy-done, bf16[256,512]{1,0:T(8,128)(2,1)} %param.5, bf16[256,512]{1,0:T(8,128)(2,1)} %param.4), kind=kOutput, calls=%fused_computation | convolution fusion | flops 3228565504 | bytes 16252928 | tf_op jit(solution)/shard_map/dot_general | solution.py:8
  9.3 16.6 %copy.7 = bf16[6144,1024]{1,0:T(8,128)(2,1)} copy(bf16[6144,1024]{0,1:T(8,128)(2,1)} %convert_bitcast_fusion) | data formatting | bytes 25165824 | tf_op jit(solution)/shard_map/convert_element_type | solution.py:12
  25.9 6.2 %copy.8 = bf16[16,48,8,1024]{3,2,0,1:T(8,128)(2,1)S(1)} copy(bf16[16,48,8,1024]{3,2,1,0:T(8,128)(2,1)} %bitcast.4) | data formatting | bytes 25165824 | tf_op jit(solution)/shard_map/reshape | solution.py:12
  32.2 299.8 %all_to_all.10 = bf16[16,48,8,1024]{3,2,0,1:T(8,128)(2,1)} all-to-all(bf16[16,48,8,1024]{3,2,0,1:T(8,128)(2,1)S(1)} %copy.8), channel_id=1, replica_groups=mesh['node'=16,'local'=48] {'local'}, dimensions={1} | all-to-all | bytes 25165824 | tf_op jit(solution)/shard_map/all_to_all | solution.py:24
  332.0 7.7 %reduce_sum.21 = bf16[16,8,1024]{2,1,0:T(8,128)(2,1)S(1)} reduce(bf16[16,48,8,1024]{3,2,0,1:T(8,128)(2,1)} %all_to_all.10, bf16[]{:T(256)} %constant.2.clone.1), dimensions={1}, to_apply=%region_0.0 | reduce | flops 6160384 | bytes 12845058 | tf_op jit(solution)/shard_map/reduce_sum | solution.py:16
  339.8 37.9 %all_to_all.11 = bf16[16,8,1024]{2,1,0:T(8,128)(2,1)S(1)} all-to-all(bf16[16,8,1024]{2,1,0:T(8,128)(2,1)S(1)} %reduce_sum.21), channel_id=1, replica_groups=mesh['node'=16,'local'=48] {'node'}, dimensions={0} | all-to-all | bytes 524288 | tf_op jit(solution)/shard_map/all_to_all | solution.py:26
  377.7 0.7 convert_reduce_fusion
Async XLA Ops:
  0.0 1.9 copy-start
where the time goes:
time: 385 us; the launch traced here: 378 us
  blocking collectives  338 us (88%)
  local copies, waits for them, and re-layouts  24.8 us (6%)
  other arithmetic  8.4 us (2%)
  matrix products  7.41 us (2%)
    all_to_all x1, blocking collectives, shards(): lax.all_to_all(parts, 'local', split_axis=1, concat_axis=1, tiled=True)  300 us
    all_to_all x1, blocking collectives, shards(): lax.all_to_all(grouped, 'node', split_axis=0, concat_axis=0, tiled=True)  37.9 us
    convert_element_type x1, local copies, waits for them, and re-layouts, local_partial(): piece.astype(jnp.bfloat16).reshape(n_node, n_local, slab, cotan.shape[1])  16.6 us
    reduce_sum x1, other arithmetic, fold_group(): return jnp.sum(received.astype(jnp.float32), axis=1).astype(jnp.bfloat16)  7.75 us

commit v1 on v0

v1 whole, which is shorter than its diff:
```python
import functools

import jax
import jax.numpy as jnp
from jax import lax
from jax.experimental import pallas as pl
from jax.experimental.pallas import tpu as pltpu
from jax.sharding import PartitionSpec as P

MESH = pl.DeviceIdType.MESH
F32, BF16 = jnp.float32, jnp.bfloat16
ROWS = 16


class Torus:
    def __init__(self, n_node, n_local, nx, ny):
        self.nx, self.ny = nx, ny
        self.zh = n_node // nx
        self.zl = n_local // (2 * ny)
        self.nz = self.zh * self.zl

    def here(self):
        node, local = lax.axis_index("node"), lax.axis_index("local")
        x, zh = node // self.zh, node % self.zh
        zl, yc = local // (2 * self.ny), local % (2 * self.ny)
        return x, yc // 2, zh * self.zl + zl, yc % 2

    def device(self, x, y, z, core):
        return (
            x * self.zh + z // self.zl,
            ((z % self.zl) * self.ny + y) * 2 + core,
        )


def kernel(
    t, half, acts_hbm, key_hbm, value_hbm, out_ref,
    acts, sib_acts, cot_own, cot_give, cot_sib, first,
    py, pz, ry, rz, y1, z1, y1r, z1r, y2, z2, y2r, z2r, fin, fin_r,
    load_sem, pair_s, pair_r, ys, yr, zs, zr,
    y1s, y1v, z1s, z1v, y2s, y2v, z2s, z2v, fin_s, fin_v,
):
    nx, ny, nz, nzh, zl = t.nx, t.ny, t.nz, t.zh, t.zl
    x, y, z, core = t.here()
    my_zh = z // zl
    tokens, width = acts.shape
    per_x = width // nx
    block = per_x // nzh

    def wrap(v, n):
        return lax.rem(v + 2 * n, n)

    def at_x(d):
        return t.device(wrap(x + d, nx), y, z, core)

    def at_y(d):
        return t.device(x, wrap(y + d, ny), z, core)

    def at_z(d):
        return t.device(x, y, wrap(z + d, nz), core)

    sibling = t.device(x, y, z, 1 - core)

    def remote(src, dst, s, r, to):
        return pltpu.make_async_remote_copy(
            src, dst, s, r, device_id=to, device_id_type=MESH
        )

    barrier = pltpu.get_barrier_semaphore()
    peers = [sibling]
    peers += [at_x(d) for d in range(1, nx)]
    peers += [at_y(d) for d in range(1, ny)]
    peers += [at_z(d) for d in range(1, nz)]
    for peer in peers:
        pl.semaphore_signal(barrier, inc=1, device_id=peer, device_id_type=MESH)

    load_acts = pltpu.make_async_copy(acts_hbm, acts, load_sem.at[0])
    load_acts.start()

    @pl.when(core == 0)
    def _():
        pltpu.make_async_copy(key_hbm, cot_own, load_sem.at[1]).start()
        pltpu.make_async_copy(value_hbm, cot_give, load_sem.at[2]).start()

    @pl.when(core == 1)
    def _():
        pltpu.make_async_copy(value_hbm, cot_own, load_sem.at[1]).start()
        pltpu.make_async_copy(key_hbm, cot_give, load_sem.at[2]).start()

    pltpu.make_async_copy(key_hbm, cot_own, load_sem.at[1]).wait()
    pltpu.make_async_copy(key_hbm, cot_give, load_sem.at[2]).wait()
    load_acts.wait()
    pl.semaphore_wait(barrier, len(peers))

    give_cot = remote(cot_give, cot_sib, pair_s.at[0], pair_r.at[0], sibling)
    give_cot.start()
    order = [wrap(my_zh + d, nzh) for d in sorted(range(nzh), key=lambda d: -min(d, nzh - d))]

    def lanes(ix, izh):
        return pl.ds(pl.multiple_of(ix * per_x + izh * block, 128), block)

    pair = []
    for k in range(nzh):
        row = []
        for ix in range(nx):
            cut = lanes(ix, order[k])
            c = remote(
                acts.at[:, cut], sib_acts.at[:, cut],
                pair_s.at[1 + k * nx + ix], pair_r.at[1 + k * nx + ix], sibling,
            )
            c.start()
            row.append(c)
        pair.append(row)

    contract = (((0,), (0,)), ((), ()))

    def own_product(i, _):
        cut = pl.ds(pl.multiple_of(i * block, 128), block)
        first[pl.ds(pl.multiple_of(i * block, 128), block), :] = lax.dot_general(
            acts[:, cut], cot_own[...], contract, preferred_element_type=F32
        )
        return 0

    lax.fori_loop(0, nx * nzh, own_product, 0)
    give_cot.wait_recv()

    def chip_product(k):
        izh = order[k]

        def one(ix, _):
            cut = lanes(ix, izh)
            rows = first[pl.ds(pl.multiple_of(ix * per_x + izh * block, 128), block), :]
            rows += lax.dot_general(
                sib_acts[:, cut], cot_sib[...], contract, preferred_element_type=F32
            )
            rows = rows.astype(BF16).reshape(zl, ny, ROWS, 2 * half)
            for j in range(zl):
                py[:, ix, izh * zl + j] = rows[j, :, :, :half]
                pz[izh * zl + j, ix] = rows[j, :, :, half:]
            return 0

        for c in pair[k]:
            c.wait_recv()
        lax.fori_loop(0, nx, one, 0)

    started = []

    def hops(axis, n, p, piece, s, first_way):
        for way in (1, -1):
            count = n // 2 if way == first_way else n // 2 - 1
            if s > count:
                continue
            d = count - s + 1
            w = 0 if way == 1 else 1
            if axis == "y":
                mine = py.at[wrap(y + way * d, ny), :, pl.ds(piece * zl, zl)]
                slot = lambda q: ry.at[w, p, q - 1]
                ssem, rsem, to = ys, yr, at_y(way)
            else:
                mine = pz.at[wrap(z + way * d, nz), pl.ds(piece * (nx // 2), nx // 2)]
                slot = lambda q: rz.at[w, p, q - 1]
                ssem, rsem, to = zs, zr, at_z(way)
            if s > 1:
                before = remote(mine, slot(s - 1), ssem.at[w, p, s - 2], rsem.at[w, p, s - 2], to)
                before.wait_recv()
                mine[...] = (mine[...].astype(F32) + slot(s - 1)[...].astype(F32)).astype(BF16)
            c = remote(mine, slot(s), ssem.at[w, p, s - 1], rsem.at[w, p, s - 1], to)
            c.start()
            started.append(c)

    events = []
    for p in range(nzh):
        lead = 1 if p % 2 == 0 else -1
        for s in range(1, ny // 2 + 1):
            events.append(((s - 1 + 0.25 * p) / (ny // 2), "y", p, s, lead))
    for p in range(2):
        lead = 1 if p == 0 else -1
        for s in range(1, nz // 2 + 1):
            events.append(((s - 1 + 0.5 * p) / (nz // 2), "z", p, s, lead))
    events.sort(key=lambda e: e[0])

    def run(e):
        _, axis, p, s, lead = e
        if axis == "y":
            hops("y", ny, p, order[p], s, lead)
        else:
            hops("z", nz, p, p, s, lead)

    for k in range(nzh):
        chip_product(k)
    for e in events:
        run(e)

    def gather_y(p):
        piece = order[p]
        cut = pl.ds(piece * zl, zl)
        total = py[y, :, cut].astype(F32)
        for w in (0, 1):
            count = ny // 2 if (w == 0) == (p % 2 == 0) else ny // 2 - 1
            if count == 0:
                continue
            slot = ry.at[w, p, count - 1]
            remote(slot, slot, ys.at[w, p, count - 1], yr.at[w, p, count - 1], sibling).wait_recv()
            total += slot[...].astype(F32)
        y1[:, cut] = total.astype(BF16)

    def gather_z(p):
        cut = pl.ds(p * (nx // 2), nx // 2)
        total = pz[z, cut].astype(F32)
        for w in (0, 1):
            count = nz // 2 if (w == 0) == (p == 0) else nz // 2 - 1
            if count == 0:
                continue
            slot = rz.at[w, p, count - 1]
            remote(slot, slot, zs.at[w, p, count - 1], zr.at[w, p, count - 1], sibling).wait_recv()
            total += slot[...].astype(F32)
        z1[cut] = total.astype(BF16)

    def send_x(src, dst, ss, rs):
        for d in range(1, nx):
            c = remote(src.at[wrap(x + d, nx)], dst.at[d - 1], ss.at[d - 1], rs, at_x(d))
            c.start()
            started.append(c)

    for p in range(nzh):
        gather_y(p)
    send_x(y1, y1r, y1s, y1v)
    for p in range(2):
        gather_z(p)
    send_x(z1, z1r, z1s, z1v)

    def wait_all(buf, sem):
        remote(buf, buf, sem, sem, sibling).wait_recv()

    def fold(mine, received, n):
        total = mine.astype(F32)
        for i in range(n):
            total += received[i].astype(F32)
        return total

    wait_all(y1r, y1v)
    y2[...] = fold(y1[x], y1r, nx - 1).astype(BF16)
    for d in range(1, nz):
        c = remote(y2.at[wrap(z + d, nz)], y2r.at[d - 1], y2s.at[d - 1], y2v, at_z(d))
        c.start()
        started.append(c)
    wait_all(z1r, z1v)
    z2[...] = fold(z1[x], z1r, nx - 1).astype(BF16)
    for d in range(1, ny):
        c = remote(z2.at[wrap(y + d, ny)], z2r.at[d - 1], z2s.at[d - 1], z2v, at_y(d))
        c.start()
        started.append(c)
    wait_all(z2r, z2v)
    fin[:, half:] = fold(z2[y], z2r, ny - 1)
    wait_all(y2r, y2v)
    fin[:, :half] = fold(y2[z], y2r, nz - 1)

    keep = ROWS // 2
    swap = remote(fin.at[pl.ds((1 - core) * keep, keep)], fin_r, fin_s, fin_v, sibling)
    swap.start()
    wide = 2 * half
    out_ref[:, pl.ds(pl.multiple_of(core * wide, 128), wide)] = fin[pl.ds(core * keep, keep), :]
    swap.wait_recv()
    out_ref[:, pl.ds(pl.multiple_of((1 - core) * wide, 128), wide)] = fin_r[...]

    give_cot.wait_send()
    for row in pair:
        for c in row:
            c.wait_send()
    for c in started:
        c.wait_send()
    swap.wait_send()


def shards(t, acts, key_cot, value_cot):
    tokens, width = acts.shape
    cols = key_cot.shape[1]
    half = cols // 2
    nx, ny, nz, nzh, zl = t.nx, t.ny, t.nz, t.zh, t.zl
    dma = pltpu.SemaphoreType.DMA
    vmem = pltpu.VMEM
    hop_y, hop_z = ny // 2, nz // 2
    scratch = [
        vmem((tokens, width), BF16), vmem((tokens, width), BF16),
        vmem((tokens, cols), BF16), vmem((tokens, cols), BF16), vmem((tokens, cols), BF16),
        vmem((width, cols), F32),
        vmem((ny, nx, nz, ROWS, half), BF16), vmem((nz, nx, ny, ROWS, half), BF16),
        vmem((2, nzh, hop_y, nx, zl, ROWS, half), BF16),
        vmem((2, 2, hop_z, nx // 2, ny, ROWS, half), BF16),
        vmem((nx, nz, ROWS, half), BF16), vmem((nx, ny, ROWS, half), BF16),
        vmem((nx - 1, nz, ROWS, half), BF16), vmem((nx - 1, ny, ROWS, half), BF16),
        vmem((nz, ROWS, half), BF16), vmem((ny, ROWS, half), BF16),
        vmem((nz - 1, ROWS, half), BF16), vmem((ny - 1, ROWS, half), BF16),
        vmem((ROWS, cols), F32), vmem((ROWS // 2, cols), F32),
        dma((3,)), dma((1 + nzh * nx,)), dma((1 + nzh * nx,)),
        dma((2, nzh, hop_y)), dma((2, nzh, hop_y)), dma((2, 2, hop_z)), dma((2, 2, hop_z)),
        dma((nx - 1,)), dma(()), dma((nx - 1,)), dma(()),
        dma((nz - 1,)), dma(()), dma((ny - 1,)), dma(()),
        dma(()), dma(()),
    ]
    anywhere = pl.BlockSpec(memory_space=pl.ANY)
    return pl.pallas_call(
        functools.partial(kernel, t, half),
        out_shape=jax.ShapeDtypeStruct((ROWS // 2, 2 * cols), F32),
        in_specs=[anywhere] * 3,
        out_specs=pl.BlockSpec(memory_space=pltpu.VMEM),
        scratch_shapes=scratch,
        compiler_params=pltpu.CompilerParams(
            collective_id=0, has_side_effects=True, vmem_limit_bytes=56 * 2**20
        ),
        cost_estimate=pl.CostEstimate(
            flops=4 * tokens * width * cols, bytes_accessed=2 * tokens * (width + 2 * cols),
            transcendentals=0,
        ),
    )(acts, key_cot, value_cot)


def solution(mesh):
    t = Torus(mesh.shape["node"], mesh.shape["local"], 4, 8)
    placed = P(("node", "local"), None)
    return jax.shard_map(
        functools.partial(shards, t), mesh=mesh, in_specs=(placed,) * 3,
        out_specs=placed, check_vma=False,
    )
```

time: 385 us -> 80.4 us (0.21); the launches traced: 378 us -> 79.8 us
  blocking collectives: 338 us -> 0 us
  Pallas kernels: 0 us -> 78.5 us
  local copies, waits for them, and re-layouts: 24.8 us -> 1.38 us
  other arithmetic: 8.4 us -> 0 us
  matrix products: 7.41 us -> 0 us
    all_to_all x2 -> x0, blocking collectives: 338 us -> none  [the longest x1 300 us: shards(): lax.all_to_all(parts, 'local', split_axis=1, concat_axis=1, tiled=True)]
    pallas_call x0 -> x1, Pallas kernels: none -> 78.5 us  [shards(): pl.pallas_call(functools.partial(kernel, t, half), out_shape=jax.ShapeDty...]
    convert_element_type x1 -> x0, local copies, waits for them, and re-layouts: 16.6 us -> none  [local_partial(): piece.astype(jnp.bfloat16).reshape(n_node, n_local, slab, cotan.shape[1])]
    reduce_sum x2 -> x0, other arithmetic: 8.4 us -> none  [the longest x1 7.75 us: fold_group(): return jnp.sum(received.astype(jnp.float32), axis=1).astype(jnp.bfloat16)]
    dot_general x1 -> x0, matrix products: 7.41 us -> none  [local_partial(): lax.dot_general(acts, cotan, (((0,), (0,)), ((), ())), preferred_element_...]
    reshape x1 -> x0, local copies, waits for them, and re-layouts: 6.24 us -> none  [local_partial(): piece.astype(jnp.bfloat16).reshape(n_node, n_local, slab, cotan.shape[1])]
where the time goes in v1:
time: 80.4 us; the launch traced here: 79.8 us
  Pallas kernels  78.5 us (98%)
  local copies, waits for them, and re-layouts  1.38 us (2%)
    pallas_call x1, Pallas kernels, shards(): pl.pallas_call(functools.partial(kernel, t, half), out_shape=jax.ShapeDty...  78.5 us

profile of v1, /device:TPU:1, one launch (start us, length us, event | category | flops | bytes accessed | tf_op | source)
XLA Modules:
  0.0 79.8 jit_solution(14097957549162467091)
XLA Ops:
  0.0 78.5 %shard_map.37 = f32[8,1024]{1,0:T(8,128)} custom-call(bf16[256,6144]{1,0:T(8,128)(2,1)} %acts_hbm.1, bf16[256,512]{1,0:T(8,128)(2,1)} %key_hbm.1, bf16[256,512]{1,0:T(8,128)(2,1)} %value_hbm.1), custom_call_target="tpu_custom_call" | custom-call | flops 3221225472 | bytes 3670016 | tf_op jit(solution)/shard_map/pallas_call | solution.py:301
  78.5 1.4 %copy.5 = f32[8,1024]{1,0:T(8,128)} copy(f32[8,1024]{1,0:T(8,128)} %shard_map.37) | data formatting | bytes 65536

commit v2 on v0

v2 whole, which is shorter than its diff:
```python
import functools
import types

import jax
import jax.numpy as jnp
from jax import lax
from jax.experimental import pallas as pl
from jax.experimental.pallas import tpu as pltpu
from jax.sharding import PartitionSpec as P

MESH = pl.DeviceIdType.MESH
F32, BF16 = jnp.float32, jnp.bfloat16
ROWS = 16
TILE = 128


class Torus:
    def __init__(self, n_node, n_local, nx, ny):
        self.nx, self.ny = nx, ny
        self.zh = n_node // nx
        self.zl = n_local // (2 * ny)
        self.nz = self.zh * self.zl

    def here(self):
        node, local = lax.axis_index("node"), lax.axis_index("local")
        x, zh = node // self.zh, node % self.zh
        zl, yc = local // (2 * self.ny), local % (2 * self.ny)
        return x, yc // 2, zh * self.zl + zl, yc % 2

    def device(self, x, y, z, core):
        return (
            x * self.zh + z // self.zl,
            ((z % self.zl) * self.ny + y) * 2 + core,
        )


def buffers(t, tokens, width, cols):
    nx, ny, nz, nzh, zl = t.nx, t.ny, t.nz, t.zh, t.zl
    dma = pltpu.SemaphoreType.DMA
    block = width // (nx * nzh)
    n2, hx, hy, hz = nzh // 2, nx // 2, ny // 2, nz // 2

    def held(*shape, dtype=BF16):
        return pltpu.VMEM(shape, dtype)

    def slab(*shape, tiles=1):
        return pltpu.VMEM((*shape, ROWS, tiles * TILE), BF16)

    return dict(
        acts=held(nzh, tokens, nx * block), sib_acts=held(nzh, tokens, nx * block),
        cot_own=held(tokens, cols), cot_give=held(tokens, cols), cot_sib=held(tokens, cols),
        first=held(nzh, nx, block, cols, dtype=F32),
        px=slab(nx, nzh, zl, ny), py=slab(ny, nzh, nx, zl), pz=slab(nz, nx, ny, tiles=2),
        rx=slab(2, 2, hx, n2, zl, ny), ry=slab(2, 2, hy, n2, nx, zl), rz=slab(2, nx, hz, ny, tiles=2),
        x1=slab(ny, nzh, zl), x1r=slab(ny - 1, nzh, zl), y1=slab(nx, nzh, zl), y1r=slab(nx - 1, nzh, zl),
        xy2=slab(nzh, zl, tiles=2), xy2r=slab(nz - 1, tiles=2),
        z1=slab(nx, ny, tiles=2), z1r=slab(nx - 1, ny, tiles=2), z2=slab(ny, tiles=2), z2r=slab(ny - 1, tiles=2),
        fin=held(ROWS, cols, dtype=F32), fin_r=held(ROWS // 2, cols, dtype=F32),
        load_sem=dma((nzh * nx + 2,)), pair_s=dma((1 + nzh,)), pair_v=dma((1 + nzh,)),
        xs=dma((2, 2, hx)), xv=dma((2, 2, hx)), ys=dma((2, 2, hy)), yv=dma((2, 2, hy)),
        zs=dma((2, nx, hz)), zv=dma((2, nx, hz)),
        x1s=dma((ny - 1,)), x1v=dma(()), y1s=dma((nx - 1,)), y1v=dma(()), xy2s=dma((nzh, zl)), xy2v=dma(()),
        z1s=dma((nx - 1,)), z1v=dma(()), z2s=dma((ny - 1,)), z2v=dma(()),
        fin_s=dma(()), fin_v=dma(()),
    )


def kernel(t, names, acts_hbm, key_hbm, value_hbm, out_ref, *refs):
    b = types.SimpleNamespace(**dict(zip(names, refs)))
    nx, ny, nz, nzh, zl = t.nx, t.ny, t.nz, t.zh, t.zl
    x, y, z, core = t.here()
    my_zh, my_zl = z // zl, z % zl
    tokens, width = acts_hbm.shape
    cols = key_hbm.shape[1]
    per_x = width // nx
    block = per_x // nzh

    def wrap(v, n):
        return lax.rem(v + 2 * n, n)

    def at(axis, d):
        if axis == "x":
            return t.device(wrap(x + d, nx), y, z, core)
        if axis == "y":
            return t.device(x, wrap(y + d, ny), z, core)
        return t.device(x, y, wrap(z + d, nz), core)

    sibling = t.device(x, y, z, 1 - core)

    def remote(src, dst, s, v, to):
        return pltpu.make_async_remote_copy(src, dst, s, v, device_id=to, device_id_type=MESH)

    started = []

    def send(src, dst, s, v, to):
        c = remote(src, dst, s, v, to)
        c.start()
        started.append(c)

    def arrived(buf, v):
        remote(buf, buf, v, v, sibling).wait_recv()

    barrier = pltpu.get_barrier_semaphore()
    peers = [sibling]
    for axis, n in (("x", nx), ("y", ny), ("z", nz)):
        peers += [at(axis, d) for d in range(1, n)]
    for peer in peers:
        pl.semaphore_signal(barrier, inc=1, device_id=peer, device_id_type=MESH)

    n_load = nzh * nx

    @pl.when(core == 0)
    def _():
        pltpu.make_async_copy(key_hbm, b.cot_own, b.load_sem.at[n_load]).start()
        pltpu.make_async_copy(value_hbm, b.cot_give, b.load_sem.at[n_load + 1]).start()

    @pl.when(core == 1)
    def _():
        pltpu.make_async_copy(value_hbm, b.cot_own, b.load_sem.at[n_load]).start()
        pltpu.make_async_copy(key_hbm, b.cot_give, b.load_sem.at[n_load + 1]).start()

    away = sorted(range(nzh), key=lambda d: -min(d, nzh - d))
    order = [wrap(my_zh + d, nzh) for d in away]
    loads = []
    for k in range(nzh):
        for ix in range(nx):
            cut = pl.ds(pl.multiple_of(ix * per_x + order[k] * block, TILE), block)
            c = pltpu.make_async_copy(
                acts_hbm.at[:, cut], b.acts.at[k, :, pl.ds(ix * block, block)], b.load_sem.at[k * nx + ix]
            )
            c.start()
            loads.append(c)

    pltpu.make_async_copy(key_hbm, b.cot_own, b.load_sem.at[n_load]).wait()
    pltpu.make_async_copy(key_hbm, b.cot_give, b.load_sem.at[n_load + 1]).wait()
    pl.semaphore_wait(barrier, len(peers))

    send(b.cot_give, b.cot_sib, b.pair_s.at[0], b.pair_v.at[0], sibling)
    for k in range(nzh):
        for c in loads[k * nx : (k + 1) * nx]:
            c.wait()
        send(b.acts.at[k], b.sib_acts.at[k], b.pair_s.at[1 + k], b.pair_v.at[1 + k], sibling)

    def dot(acts, k, ix, cot):
        cut = pl.ds(pl.multiple_of(ix * block, TILE), block)
        return lax.dot_general(
            acts[k, :, cut], cot[...], (((0,), (0,)), ((), ())), preferred_element_type=F32
        )

    def own_product(k):
        def one(ix, _):
            b.first[k, ix] = dot(b.acts, k, ix, b.cot_own)
            return 0

        lax.fori_loop(0, nx, one, 0)

    def chip_product(k):
        izh = order[k]

        def one(ix, _):
            rows = b.first[k, ix] + dot(b.sib_acts, k, ix, b.cot_sib)
            rows = rows.astype(BF16).reshape(zl, ny, ROWS, cols)
            b.px[ix, k] = rows[..., :TILE]
            for j in range(zl):
                b.py[:, k, ix, j] = rows[j, :, :, TILE : 2 * TILE]
            b.pz[pl.ds(izh * zl, zl), ix] = rows[..., 2 * TILE :]
            return 0

        if k == 0:
            arrived(b.cot_sib, b.pair_v.at[0])
        arrived(b.sib_acts.at[k], b.pair_v.at[1 + k])
        lax.fori_loop(0, nx, one, 0)

    n2 = nzh // 2

    def ring(axis, p):
        if axis == "x":
            return (
                nx, x, lambda to: b.px.at[to, pl.ds(p * n2, n2)], lambda w, q: b.rx.at[w, p, q],
                lambda w, q: (b.xs.at[w, p, q], b.xv.at[w, p, q]), p,
            )
        if axis == "y":
            return (
                ny, y, lambda to: b.py.at[to, pl.ds(p * n2, n2)], lambda w, q: b.ry.at[w, p, q],
                lambda w, q: (b.ys.at[w, p, q], b.yv.at[w, p, q]), p,
            )
        return (
            nz, z, lambda to: b.pz.at[to, p], lambda w, q: b.rz.at[w, p, q],
            lambda w, q: (b.zs.at[w, p, q], b.zv.at[w, p, q]), 0 if p < nx // 2 else 1,
        )

    def count(n, w, long_way):
        return n // 2 if w == long_way else n // 2 - 1

    def hop(axis, p, w, s):
        n, me, sums, slot, sems, long_way = ring(axis, p)
        hops, way = count(n, w, long_way), 1 - 2 * w
        if s > hops:
            return
        mine = sums(wrap(me + way * (hops - s + 1), n))
        if s > 1:
            arrived(slot(w, s - 2), sems(w, s - 2)[1])
            mine[...] = (mine[...].astype(F32) + slot(w, s - 2)[...].astype(F32)).astype(BF16)
        send(mine, slot(w, s - 1), *sems(w, s - 1), at(axis, way))

    def gathered(axis, p):
        n, me, sums, slot, sems, long_way = ring(axis, p)
        total = sums(me)[...].astype(F32)
        for w in (0, 1):
            hops = count(n, w, long_way)
            if hops > 0:
                arrived(slot(w, hops - 1), sems(w, hops - 1)[1])
                total += slot(w, hops - 1)[...].astype(F32)
        return total.astype(BF16)

    def fold(mine, received, n):
        total = mine.astype(F32)
        for i in range(n):
            total += received[i].astype(F32)
        return total

    def to_line(axis, n, me, src, dst, ss, v):
        for d in range(1, n):
            send(src.at[wrap(me + d, n)], dst.at[d - 1], ss.at[d - 1], v, at(axis, d))

    def gather_x():
        for p in (0, 1):
            rows = gathered("x", p)
            for g in range(n2):
                for j in range(zl):
                    b.x1[:, p * n2 + g, j] = rows[g, j]
        to_line("y", ny, y, b.x1, b.x1r, b.x1s, b.x1v)

    def gather_y():
        for p in (1, 0):
            rows = gathered("y", p)
            for g in range(n2):
                b.y1[:, p * n2 + g] = rows[g]
        to_line("x", nx, x, b.y1, b.y1r, b.y1s, b.y1v)

    def fold_x():
        arrived(b.x1r, b.x1v)
        b.xy2[:, :, :, :TILE] = fold(b.x1[y], b.x1r, ny - 1).astype(BF16)

    def fold_y():
        arrived(b.y1r, b.y1v)
        b.xy2[:, :, :, TILE:] = fold(b.y1[x], b.y1r, nx - 1).astype(BF16)
        for k in range(nzh):
            own = away[k] == 0
            for j in range(zl - 1 if own else zl):
                row = lax.rem(my_zl + 1 + j, zl) if own else j
                to = order[k] * zl + row
                send(
                    b.xy2.at[k, row], b.xy2r.at[wrap(to - z, nz) - 1], b.xy2s.at[k, j], b.xy2v,
                    t.device(x, y, to, core),
                )

    def gather_z():
        for p in [*range(nx // 2, nx), *range(nx // 2)]:
            b.z1[p] = gathered("z", p)
        to_line("x", nx, x, b.z1, b.z1r, b.z1s, b.z1v)

    def fold_z():
        arrived(b.z1r, b.z1v)
        b.z2[...] = fold(b.z1[x], b.z1r, nx - 1).astype(BF16)
        to_line("y", ny, y, b.z2, b.z2r, b.z2s, b.z2v)

    def drain():
        for c in started:
            c.wait_send()
        started.clear()

    def end_xy():
        arrived(b.xy2r, b.xy2v)
        b.fin[:, : 2 * TILE] = fold(b.xy2[nzh - 1, my_zl], b.xy2r, nz - 1)

    def end_z():
        arrived(b.z2r, b.z2v)
        b.fin[:, 2 * TILE :] = fold(b.z2[y], b.z2r, ny - 1)

    events = []

    def add(time, f, *args):
        events.append((time, functools.partial(f, *args)))

    ready = [2.5 + 1.5 * k for k in range(nzh)]
    for k in range(nzh):
        add(1.5 * k, own_product, k)
        add(ready[k], chip_product, k)
    most = ready[max(nzh - 2, 0)]
    for w in (0, 1):
        for p in (0, 1):
            half = ready[n2 - 1 if p == 0 else nzh - 1] + 0.1
            for s in range(1, nx // 2 + 1):
                add(half + 7.5 * (s - 1) + 0.1, hop, "x", p, w, s)
            for s in range(1, ny // 2 + 1):
                add(half + 5.1 * (s - 1), hop, "y", p, w, s)
        for p in range(nx):
            first = ready[0] + 0.1 if w == (0 if p < nx // 2 else 1) else most + 0.2
            for s in range(1, nz // 2 + 1):
                add(first + 5.1 * (s - 1) + 0.01 * p, hop, "z", p, w, s)
    add(22.0, gather_x)
    add(25.0, gather_y)
    add(27.5, fold_x)
    add(30.0, fold_y)
    add(33.4, gather_z)
    add(37.5, fold_z)
    add(38.0, drain)
    add(40.0, end_xy)
    add(42.0, end_z)
    for _, step in sorted(events, key=lambda e: e[0]):
        step()

    keep = ROWS // 2
    send(b.fin.at[pl.ds((1 - core) * keep, keep)], b.fin_r, b.fin_s, b.fin_v, sibling)
    out_ref[:, pl.ds(pl.multiple_of(core * cols, TILE), cols)] = b.fin[pl.ds(core * keep, keep), :]
    arrived(b.fin_r, b.fin_v)
    out_ref[:, pl.ds(pl.multiple_of((1 - core) * cols, TILE), cols)] = b.fin_r[...]
    drain()


def shards(t, acts, key_cot, value_cot):
    tokens, width = acts.shape
    cols = key_cot.shape[1]
    held = buffers(t, tokens, width, cols)
    anywhere = pl.BlockSpec(memory_space=pl.ANY)
    return pl.pallas_call(
        functools.partial(kernel, t, tuple(held)),
        out_shape=jax.ShapeDtypeStruct((ROWS // 2, 2 * cols), F32),
        in_specs=[anywhere] * 3,
        out_specs=pl.BlockSpec(memory_space=pltpu.VMEM),
        scratch_shapes=list(held.values()),
        compiler_params=pltpu.CompilerParams(
            collective_id=0, has_side_effects=True, vmem_limit_bytes=56 * 2**20
        ),
        cost_estimate=pl.CostEstimate(
            flops=4 * tokens * width * cols, bytes_accessed=2 * tokens * (width + 2 * cols),
            transcendentals=0,
        ),
    )(acts, key_cot, value_cot)


def solution(mesh):
    t = Torus(mesh.shape["node"], mesh.shape["local"], 4, 8)
    placed = P(("node", "local"), None)
    return jax.shard_map(
        functools.partial(shards, t), mesh=mesh, in_specs=(placed,) * 3,
        out_specs=placed, check_vma=False,
    )
```

time: 385 us -> 82.1 us (0.21); the launches traced: 378 us -> 81.9 us
  blocking collectives: 338 us -> 0 us
  Pallas kernels: 0 us -> 80.5 us
  local copies, waits for them, and re-layouts: 24.8 us -> 1.38 us
  other arithmetic: 8.4 us -> 0 us
  matrix products: 7.41 us -> 0 us
    all_to_all x2 -> x0, blocking collectives: 338 us -> none  [the longest x1 300 us: shards(): lax.all_to_all(parts, 'local', split_axis=1, concat_axis=1, tiled=True)]
    pallas_call x0 -> x1, Pallas kernels: none -> 80.5 us  [shards(): pl.pallas_call(functools.partial(kernel, t, tuple(held)), out_shape=jax.S...]
    convert_element_type x1 -> x0, local copies, waits for them, and re-layouts: 16.6 us -> none  [local_partial(): piece.astype(jnp.bfloat16).reshape(n_node, n_local, slab, cotan.shape[1])]
    reduce_sum x2 -> x0, other arithmetic: 8.4 us -> none  [the longest x1 7.75 us: fold_group(): return jnp.sum(received.astype(jnp.float32), axis=1).astype(jnp.bfloat16)]
    dot_general x1 -> x0, matrix products: 7.41 us -> none  [local_partial(): lax.dot_general(acts, cotan, (((0,), (0,)), ((), ())), preferred_element_...]
    reshape x1 -> x0, local copies, waits for them, and re-layouts: 6.24 us -> none  [local_partial(): piece.astype(jnp.bfloat16).reshape(n_node, n_local, slab, cotan.shape[1])]
where the time goes in v2:
time: 82.1 us; the launch traced here: 81.9 us
  Pallas kernels  80.5 us (98%)
  local copies, waits for them, and re-layouts  1.38 us (2%)
    pallas_call x1, Pallas kernels, shards(): pl.pallas_call(functools.partial(kernel, t, tuple(held)), out_shape=jax.S...  80.5 us

profile of v2, /device:TPU:1, one launch (start us, length us, event | category | flops | bytes accessed | tf_op | source)
XLA Modules:
  0.0 81.9 jit_solution(12600709955004968488)
XLA Ops:
  0.0 80.5 %shard_map.37 = f32[8,1024]{1,0:T(8,128)} custom-call(bf16[256,6144]{1,0:T(8,128)(2,1)} %acts_hbm.1, bf16[256,512]{1,0:T(8,128)(2,1)} %key_hbm.1, bf16[256,512]{1,0:T(8,128)(2,1)} %value_hbm.1), custom_call_target="tpu_custom_call" | custom-call | flops 3221225472 | bytes 3670016 | tf_op jit(solution)/shard_map/pallas_call | solution.py:327
  80.5 1.4 %copy.5 = f32[8,1024]{1,0:T(8,128)} copy(f32[8,1024]{1,0:T(8,128)} %shard_map.37) | data formatting | bytes 65536

commit v3 on v2

v3 whole, which is shorter than its diff:
```python
import functools
import types

import jax
import jax.numpy as jnp
from jax import lax
from jax.experimental import pallas as pl
from jax.experimental.pallas import tpu as pltpu
from jax.sharding import PartitionSpec as P

MESH = pl.DeviceIdType.MESH
F32, BF16 = jnp.float32, jnp.bfloat16
ROWS = 16
TILE = 128


class Torus:
    def __init__(self, n_node, n_local, nx, ny):
        self.nx, self.ny = nx, ny
        self.zh = n_node // nx
        self.zl = n_local // (2 * ny)
        self.nz = self.zh * self.zl

    def here(self):
        node, local = lax.axis_index("node"), lax.axis_index("local")
        x, zh = node // self.zh, node % self.zh
        zl, yc = local // (2 * self.ny), local % (2 * self.ny)
        return x, yc // 2, zh * self.zl + zl, yc % 2

    def device(self, x, y, z, core):
        return (
            x * self.zh + z // self.zl,
            ((z % self.zl) * self.ny + y) * 2 + core,
        )


def buffers(t, tokens, width, cols):
    nx, ny, nz = t.nx, t.ny, t.nz
    dma = pltpu.SemaphoreType.DMA
    n2, hx, hy, hz = nz // 2, nx // 2, ny // 2, nz // 2

    def held(*shape, dtype=BF16):
        return pltpu.VMEM(shape, dtype)

    def slab(*shape, tiles=1):
        return pltpu.VMEM((*shape, ROWS, tiles * TILE), BF16)

    return dict(
        acts=held(nx, tokens, width // nx), sib_acts=held(nx, tokens, width // nx),
        cot_own=held(tokens, cols), cot_give=held(tokens, cols), cot_sib=held(tokens, cols),
        first=held(nz, width // nz, cols, dtype=F32),
        px=slab(nx, nz, ny), py=slab(ny, nz, nx), pz=slab(nz, nx, ny, tiles=2),
        rx=slab(2, 2, hx, n2, ny), ry=slab(2, 2, hy, n2, nx), rz=slab(2, nx, hz, ny, tiles=2),
        x1=slab(2, ny, n2), x1r=slab(2, ny - 1, n2), y1=slab(nx, nz), y1r=slab(nx - 1, nz),
        xy2=slab(nz, tiles=2), xy2r=slab(nz - 1, tiles=2),
        z1=slab(nx, ny, tiles=2), z1r=slab(nx - 1, ny, tiles=2), z2=slab(ny, tiles=2), z2r=slab(ny - 1, tiles=2),
        fin=held(ROWS, cols, dtype=F32), fin_r=held(ROWS // 2, cols, dtype=F32),
        load_sem=dma((nx + 2,)), pair_s=dma((1 + nz,)), pair_v=dma((1 + nz,)),
        xs=dma((2, 2, hx)), xv=dma((2, 2, hx)), ys=dma((2, 2, hy)), yv=dma((2, 2, hy)),
        zs=dma((2, nx, hz)), zv=dma((2, nx, hz)),
        x1s=dma((2, ny - 1)), x1v=dma((2,)), y1s=dma((nx - 1,)), y1v=dma(()), xy2s=dma((nz - 1,)), xy2v=dma(()),
        z1s=dma((nx - 1,)), z1v=dma(()), z2s=dma((ny - 1,)), z2v=dma(()),
        fin_s=dma(()), fin_v=dma(()),
    )


def kernel(t, names, acts_hbm, key_hbm, value_hbm, out_ref, *refs):
    b = types.SimpleNamespace(**dict(zip(names, refs)))
    nx, ny, nz = t.nx, t.ny, t.nz
    x, y, z, core = t.here()
    tokens, width = acts_hbm.shape
    cols = key_hbm.shape[1]
    per_x = width // nx
    block = per_x // nz

    def wrap(v, n):
        return lax.rem(v + 2 * n, n)

    @functools.cache
    def at(axis, d):
        if axis == "x":
            return t.device(wrap(x + d, nx), y, z, core)
        if axis == "y":
            return t.device(x, wrap(y + d, ny), z, core)
        return t.device(x, y, wrap(z + d, nz), core)

    sibling = t.device(x, y, z, 1 - core)

    def remote(src, dst, s, v, to):
        return pltpu.make_async_remote_copy(src, dst, s, v, device_id=to, device_id_type=MESH)

    started = []

    def send(src, dst, s, v, to):
        c = remote(src, dst, s, v, to)
        c.start()
        started.append(c)

    def arrived(buf, v):
        remote(buf, buf, v, v, sibling).wait_recv()

    barrier = pltpu.get_barrier_semaphore()
    peers = [sibling]
    for axis, n in (("x", nx), ("y", ny), ("z", nz)):
        peers += [at(axis, d) for d in range(1, n)]
    for peer in peers:
        pl.semaphore_signal(barrier, inc=1, device_id=peer, device_id_type=MESH)

    n_load = nx

    @pl.when(core == 0)
    def _():
        pltpu.make_async_copy(key_hbm, b.cot_own, b.load_sem.at[n_load]).start()
        pltpu.make_async_copy(value_hbm, b.cot_give, b.load_sem.at[n_load + 1]).start()

    @pl.when(core == 1)
    def _():
        pltpu.make_async_copy(value_hbm, b.cot_own, b.load_sem.at[n_load]).start()
        pltpu.make_async_copy(key_hbm, b.cot_give, b.load_sem.at[n_load + 1]).start()

    loads = []
    for ix in range(nx):
        c = pltpu.make_async_copy(
            acts_hbm.at[:, pl.ds(ix * per_x, per_x)], b.acts.at[ix], b.load_sem.at[ix]
        )
        c.start()
        loads.append(c)

    pltpu.make_async_copy(key_hbm, b.cot_own, b.load_sem.at[n_load]).wait()
    pltpu.make_async_copy(key_hbm, b.cot_give, b.load_sem.at[n_load + 1]).wait()
    for c in loads:
        c.wait()
    pl.semaphore_wait(barrier, len(peers))

    offs = [nz // 2]
    for d in range(nz // 2 - 1, 0, -1):
        offs += [d, -d]
    offs.append(0)

    def cut(i):
        return pl.ds(pl.multiple_of(wrap(z + offs[i], nz) * block, TILE), block)

    send(b.cot_give, b.cot_sib, b.pair_s.at[0], b.pair_v.at[0], sibling)
    for i in range(nz):
        part = (slice(None), slice(None), cut(i))
        send(b.acts.at[part], b.sib_acts.at[part], b.pair_s.at[1 + i], b.pair_v.at[1 + i], sibling)

    def dot(acts, i, cot):
        rows = jnp.concatenate([acts[ix, :, cut(i)] for ix in range(nx)], axis=1)
        return lax.dot_general(
            rows, cot[...], (((0,), (0,)), ((), ())), preferred_element_type=F32
        )

    def own_product(i):
        b.first[i] = dot(b.acts, i, b.cot_own)

    def chip_product(i):
        if i == 0:
            arrived(b.cot_sib, b.pair_v.at[0])
        arrived(b.sib_acts.at[:, :, cut(i)], b.pair_v.at[1 + i])
        rows = b.first[i] + dot(b.sib_acts, i, b.cot_sib)
        rows = rows.astype(BF16).reshape(nx, ny, ROWS, cols)
        b.px[:, i] = rows[..., :TILE]
        for ix in range(nx):
            b.py[:, i, ix] = rows[ix, :, :, TILE : 2 * TILE]
        b.pz[i] = rows[..., 2 * TILE :]

    n2 = nz // 2

    def ring(axis, p):
        half = pl.ds(p * n2, n2)
        if axis == "x":
            return (
                nx, lambda d: b.px.at[wrap(x + d, nx), half], lambda w, q: b.rx.at[w, p, q],
                lambda w, q: (b.xs.at[w, p, q], b.xv.at[w, p, q]), p,
            )
        if axis == "y":
            return (
                ny, lambda d: b.py.at[wrap(y + d, ny), half], lambda w, q: b.ry.at[w, p, q],
                lambda w, q: (b.ys.at[w, p, q], b.yv.at[w, p, q]), p,
            )
        return (
            nz, lambda d: b.pz.at[offs.index(n2 if d == -n2 else d), p], lambda w, q: b.rz.at[w, p, q],
            lambda w, q: (b.zs.at[w, p, q], b.zv.at[w, p, q]), 0 if p < nx // 2 else 1,
        )

    def count(n, w, long_way):
        return n // 2 if w == long_way else n // 2 - 1

    def hop(axis, p, w, s):
        n, sums, slot, sems, long_way = ring(axis, p)
        hops, way = count(n, w, long_way), 1 - 2 * w
        if s > hops:
            return
        mine = sums(way * (hops - s + 1))
        if s > 1:
            arrived(slot(w, s - 2), sems(w, s - 2)[1])
            mine[...] = (mine[...].astype(F32) + slot(w, s - 2)[...].astype(F32)).astype(BF16)
        send(mine, slot(w, s - 1), *sems(w, s - 1), at(axis, way))

    def gathered(axis, p):
        n, sums, slot, sems, long_way = ring(axis, p)
        total = sums(0)[...].astype(F32)
        for w in (0, 1):
            hops = count(n, w, long_way)
            if hops > 0:
                arrived(slot(w, hops - 1), sems(w, hops - 1)[1])
                total += slot(w, hops - 1)[...].astype(F32)
        return total.astype(BF16)

    def fold(mine, received, n):
        total = mine.astype(F32)
        for i in range(n):
            total += received[i].astype(F32)
        return total

    def to_line(axis, n, me, src, dst, ss, v):
        for d in range(1, n):
            send(src.at[wrap(me + d, n)], dst.at[d - 1], ss.at[d - 1], v, at(axis, d))

    def gather_x(p):
        rows = gathered("x", p)
        for g in range(n2):
            b.x1[p, :, g] = rows[g]
        to_line("y", ny, y, b.x1.at[p], b.x1r.at[p], b.x1s.at[p], b.x1v.at[p])

    def gather_y():
        for p in (1, 0):
            rows = gathered("y", p)
            for g in range(n2):
                b.y1[:, p * n2 + g] = rows[g]
        to_line("x", nx, x, b.y1, b.y1r, b.y1s, b.y1v)

    def fold_x(p):
        arrived(b.x1r.at[p], b.x1v.at[p])
        b.xy2[p * n2 : (p + 1) * n2, :, :TILE] = fold(b.x1[p, y], b.x1r.at[p], ny - 1).astype(BF16)

    def fold_y():
        arrived(b.y1r, b.y1v)
        b.xy2[:, :, TILE:] = fold(b.y1[x], b.y1r, nx - 1).astype(BF16)
        for i in range(nz - 1):
            send(b.xy2.at[i], b.xy2r.at[offs[i] % nz - 1], b.xy2s.at[i], b.xy2v, at("z", offs[i] % nz))

    def gather_z():
        for p in [*range(nx // 2, nx), *range(nx // 2)]:
            b.z1[p] = gathered("z", p)
        to_line("x", nx, x, b.z1, b.z1r, b.z1s, b.z1v)

    def fold_z():
        arrived(b.z1r, b.z1v)
        b.z2[...] = fold(b.z1[x], b.z1r, nx - 1).astype(BF16)
        to_line("y", ny, y, b.z2, b.z2r, b.z2s, b.z2v)

    def drain():
        for c in started:
            c.wait_send()
        started.clear()

    def end_xy():
        arrived(b.xy2r, b.xy2v)
        b.fin[:, : 2 * TILE] = fold(b.xy2[nz - 1], b.xy2r, nz - 1)

    def end_z():
        arrived(b.z2r, b.z2v)
        b.fin[:, 2 * TILE :] = fold(b.z2[y], b.z2r, ny - 1)

    events = []

    def add(time, f, *args):
        events.append((time, functools.partial(f, *args)))

    ready = [2.2 + 0.5 * i for i in range(nz)]
    for i in range(nz):
        add(0.0 if i < 2 else ready[i - 2] + 0.2, own_product, i)
        add(ready[i], chip_product, i)
    for w in (0, 1):
        for p in (0, 1):
            half = ready[(p + 1) * n2 - 1] + 0.1
            for s in range(1, nx // 2 + 1):
                add(half + 7.2 * (s - 1) + 0.1, hop, "x", p, w, s)
            for s in range(1, ny // 2 + 1):
                add(half + 5.1 * (s - 1), hop, "y", p, w, s)
        for p in range(nx):
            begin = ready[0] + 0.1 if w == (0 if p < nx // 2 else 1) else ready[min(2, nz - 1)] + 0.1
            for s in range(1, nz // 2 + 1):
                add(begin + (5.1 if begin < ready[0] + 0.2 else 5.5) * (s - 1) + 0.01 * p, hop, "z", p, w, s)
    add(19.0, gather_x, 0)
    add(22.5, gather_x, 1)
    add(26.0, gather_y)
    add(31.0, fold_x, 0)
    add(31.1, fold_x, 1)
    add(31.2, fold_y)
    add(33.0, gather_z)
    add(33.1, drain)
    add(37.0, fold_z)
    add(40.0, end_xy)
    add(42.0, end_z)
    for _, step in sorted(events, key=lambda e: e[0]):
        step()

    keep = ROWS // 2
    send(b.fin.at[pl.ds((1 - core) * keep, keep)], b.fin_r, b.fin_s, b.fin_v, sibling)
    out_ref[:, pl.ds(pl.multiple_of(core * cols, TILE), cols)] = b.fin[pl.ds(core * keep, keep), :]
    arrived(b.fin_r, b.fin_v)
    out_ref[:, pl.ds(pl.multiple_of((1 - core) * cols, TILE), cols)] = b.fin_r[...]
    drain()


def shards(t, acts, key_cot, value_cot):
    tokens, width = acts.shape
    cols = key_cot.shape[1]
    held = buffers(t, tokens, width, cols)
    anywhere = pl.BlockSpec(memory_space=pl.ANY)
    return pl.pallas_call(
        functools.partial(kernel, t, tuple(held)),
        out_shape=jax.ShapeDtypeStruct((ROWS // 2, 2 * cols), F32),
        in_specs=[anywhere] * 3,
        out_specs=pl.BlockSpec(memory_space=pltpu.VMEM),
        scratch_shapes=list(held.values()),
        compiler_params=pltpu.CompilerParams(
            collective_id=0, has_side_effects=True, vmem_limit_bytes=56 * 2**20
        ),
        cost_estimate=pl.CostEstimate(
            flops=4 * tokens * width * cols, bytes_accessed=2 * tokens * (width + 2 * cols),
            transcendentals=0,
        ),
    )(acts, key_cot, value_cot)


def solution(mesh):
    t = Torus(mesh.shape["node"], mesh.shape["local"], 4, 8)
    placed = P(("node", "local"), None)
    return jax.shard_map(
        functools.partial(shards, t), mesh=mesh, in_specs=(placed,) * 3,
        out_specs=placed, check_vma=False,
    )
```

time: 82.1 us -> 73 us (0.89)
  Pallas kernels: 80.5 us -> 71.4 us
    pallas_call x1, Pallas kernels: 80.5 us -> 71.4 us  [shards(): pl.pallas_call(functools.partial(kernel, t, tuple(held)), out_shape=jax.S...]
where the time goes in v3:
time: 73 us; the launch traced here: 72.8 us
  Pallas kernels  71.4 us (98%)
  local copies, waits for them, and re-layouts  1.38 us (2%)
    pallas_call x1, Pallas kernels, shards(): pl.pallas_call(functools.partial(kernel, t, tuple(held)), out_shape=jax.S...  71.4 us

profile of v3, /device:TPU:1, one launch (start us, length us, event | category | flops | bytes accessed | tf_op | source)
XLA Modules:
  0.0 72.8 jit_solution(6432141000925266080)
XLA Ops:
  0.0 71.4 %shard_map.37 = f32[8,1024]{1,0:T(8,128)} custom-call(bf16[256,6144]{1,0:T(8,128)(2,1)} %acts_hbm.1, bf16[256,512]{1,0:T(8,128)(2,1)} %key_hbm.1, bf16[256,512]{1,0:T(8,128)(2,1)} %value_hbm.1), custom_call_target="tpu_custom_call" | custom-call | flops 3221225472 | bytes 3670016 | tf_op jit(solution)/shard_map/pallas_call | solution.py:314
  71.4 1.4 %copy.5 = f32[8,1024]{1,0:T(8,128)} copy(f32[8,1024]{1,0:T(8,128)} %shard_map.37) | data formatting | bytes 65536

commit v4 on v0

v4 whole, which is shorter than its diff:
```python
import functools
import types

import jax
import jax.numpy as jnp
from jax import lax
from jax.experimental import pallas as pl
from jax.experimental.pallas import tpu as pltpu
from jax.sharding import PartitionSpec as P

MESH = pl.DeviceIdType.MESH
F32, BF16 = jnp.float32, jnp.bfloat16
ROWS = 16
TILE = 128


class Torus:
    def __init__(self, n_node, n_local, nx, ny):
        self.nx, self.ny = nx, ny
        self.zh = n_node // nx
        self.zl = n_local // (2 * ny)
        self.nz = self.zh * self.zl

    def here(self):
        node, local = lax.axis_index("node"), lax.axis_index("local")
        x, zh = node // self.zh, node % self.zh
        zl, yc = local // (2 * self.ny), local % (2 * self.ny)
        return x, yc // 2, zh * self.zl + zl, yc % 2

    def device(self, x, y, z, core):
        return (
            x * self.zh + z // self.zl,
            ((z % self.zl) * self.ny + y) * 2 + core,
        )


def shared_buffers(t, tokens, width, cols):
    nx, nz = t.nx, t.nz
    dma = pltpu.SemaphoreType.DMA

    def held(*shape, dtype=BF16):
        return pltpu.VMEM(shape, dtype)

    return dict(
        acts=held(nx, tokens, width // nx), sib_acts=held(nx, tokens, width // nx),
        cot_own=held(tokens, cols), cot_give=held(tokens, cols), cot_sib=held(tokens, cols),
        first=held(nz, width // nz, cols, dtype=F32),
        fin=held(ROWS, cols, dtype=F32), fin_r=held(ROWS // 2, cols, dtype=F32),
        load_sem=dma((nx + 2,)), pair_s=dma((1 + nz,)), pair_v=dma((1 + nz,)),
        fin_s=dma(()), fin_v=dma(()),
    )


def core_buffers(t, xt, zt):
    nx, ny, nz = t.nx, t.ny, t.nz
    dma = pltpu.SemaphoreType.DMA
    n2, hx, hy, hz = nz // 2, nx // 2, ny // 2, nz // 2

    def slab(*shape, tiles=1):
        return pltpu.VMEM((*shape, ROWS, tiles * TILE), BF16)

    return dict(
        px=slab(nx, nz, ny, tiles=xt), py=slab(ny, nz, nx), pz=slab(nz, nx, ny, tiles=zt),
        rx=slab(2, 2, hx, n2, ny, tiles=xt), ry=slab(2, 2, hy, n2, nx), rz=slab(2, nx, hz, ny, tiles=zt),
        x1=slab(ny, n2, tiles=xt), x1r=slab(ny - 1, n2, tiles=xt),
        xn=slab(n2, ny, tiles=xt), xnr=slab(max(n2 - 1, 1), ny, tiles=xt),
        y1=slab(nx, nz), y1r=slab(nx - 1, nz),
        far=slab(n2, tiles=xt + 1), far_r=slab(n2, tiles=xt + 1), near=slab(n2), near_r=slab(max(n2 - 1, 1)),
        z1=slab(nx, ny, tiles=zt), z1r=slab(nx - 1, ny, tiles=zt), z2=slab(ny, tiles=zt + xt), z2r=slab(ny - 1, tiles=zt + xt),
        xs=dma((2, 2, hx)), xv=dma((2, 2, hx)), ys=dma((2, 2, hy)), yv=dma((2, 2, hy)),
        zs=dma((2, nx, hz)), zv=dma((2, nx, hz)),
        x1s=dma((ny - 1,)), x1v=dma(()), y1s=dma((nx - 1,)), y1v=dma(()), xns=dma((n2,)), xnv=dma(()),
        far_s=dma((n2,)), far_v=dma(()), near_s=dma((n2,)), near_v=dma(()),
        z1s=dma((nx - 1,)), z1v=dma(()), z2s=dma((ny - 1,)), z2v=dma(()),
    )


SHARES = ((2, 1), (1, 2))


def kernel(t, names, acts_hbm, key_hbm, value_hbm, out_ref, *refs):
    held = dict(zip(names, refs))
    b = types.SimpleNamespace(**{n: r for (c, n), r in held.items() if c is None})
    nx, ny, nz = t.nx, t.ny, t.nz
    x, y, z, core = t.here()
    tokens, width = acts_hbm.shape
    cols = key_hbm.shape[1]
    per_x = width // nx
    block = per_x // nz

    def wrap(v, n):
        return lax.rem(v + 2 * n, n)

    line = {("x", d): t.device(wrap(x + d, nx), y, z, core) for d in range(1, nx)}
    line.update({("y", d): t.device(x, wrap(y + d, ny), z, core) for d in range(1, ny)})
    line.update({("z", d): t.device(x, y, wrap(z + d, nz), core) for d in range(1, nz)})
    size = {"x": nx, "y": ny, "z": nz}

    def at(axis, d):
        return line[axis, d % size[axis]]

    sibling = t.device(x, y, z, 1 - core)

    def remote(src, dst, s, v, to):
        return pltpu.make_async_remote_copy(src, dst, s, v, device_id=to, device_id_type=MESH)

    started = []

    def send(src, dst, s, v, to):
        c = remote(src, dst, s, v, to)
        c.start()
        started.append(c)

    def arrived(buf, v):
        remote(buf, buf, v, v, sibling).wait_recv()

    barrier = pltpu.get_barrier_semaphore()
    peers = [sibling] + [line[a, d] for a, n in size.items() for d in sorted({1, n - 1})]
    for peer in peers:
        pl.semaphore_signal(barrier, inc=1, device_id=peer, device_id_type=MESH)

    n_load = nx

    @pl.when(core == 0)
    def _():
        pltpu.make_async_copy(key_hbm, b.cot_own, b.load_sem.at[n_load]).start()
        pltpu.make_async_copy(value_hbm, b.cot_give, b.load_sem.at[n_load + 1]).start()

    @pl.when(core == 1)
    def _():
        pltpu.make_async_copy(value_hbm, b.cot_own, b.load_sem.at[n_load]).start()
        pltpu.make_async_copy(key_hbm, b.cot_give, b.load_sem.at[n_load + 1]).start()

    loads = []
    for ix in range(nx):
        c = pltpu.make_async_copy(
            acts_hbm.at[:, pl.ds(ix * per_x, per_x)], b.acts.at[ix], b.load_sem.at[ix]
        )
        c.start()
        loads.append(c)

    pltpu.make_async_copy(key_hbm, b.cot_own, b.load_sem.at[n_load]).wait()
    pltpu.make_async_copy(key_hbm, b.cot_give, b.load_sem.at[n_load + 1]).wait()
    for c in loads:
        c.wait()
    pl.semaphore_wait(barrier, len(peers))

    offs = [nz // 2]
    for d in range(nz // 2 - 1, 0, -1):
        offs += [d, -d]
    offs.append(0)

    def cut(i):
        return pl.ds(pl.multiple_of(wrap(z + offs[i], nz) * block, TILE), block)

    send(b.cot_give, b.cot_sib, b.pair_s.at[0], b.pair_v.at[0], sibling)
    for i in range(nz):
        part = (slice(None), slice(None), cut(i))
        send(b.acts.at[part], b.sib_acts.at[part], b.pair_s.at[1 + i], b.pair_v.at[1 + i], sibling)

    def work(c):
        mine = list(started)

        def send(*args):
            copy = remote(*args)
            copy.start()
            mine.append(copy)

        b = types.SimpleNamespace(**{n: r for (of, n), r in held.items() if of in (None, c)})
        to_y = SHARES[c][0] * TILE
        to_z = to_y + TILE

        def dot(acts, i, cot):
            rows = jnp.concatenate([acts[ix, :, cut(i)] for ix in range(nx)], axis=1)
            return lax.dot_general(
                rows, cot[...], (((0,), (0,)), ((), ())), preferred_element_type=F32
            )

        def own_product(i):
            b.first[i] = dot(b.acts, i, b.cot_own)

        def chip_product(i):
            if i == 0:
                arrived(b.cot_sib, b.pair_v.at[0])
            arrived(b.sib_acts.at[:, :, cut(i)], b.pair_v.at[1 + i])
            rows = b.first[i] + dot(b.sib_acts, i, b.cot_sib)
            rows = rows.astype(BF16).reshape(nx, ny, ROWS, cols)
            b.px[:, i] = rows[..., :to_y]
            for ix in range(nx):
                b.py[:, i, ix] = rows[ix, :, :, to_y:to_z]
            b.pz[i] = rows[..., to_z:]

        n2 = nz // 2

        def ring(axis, p):
            half = pl.ds(p * n2, n2)
            if axis == "x":
                return (
                    nx, lambda d: b.px.at[wrap(x + d, nx), half], lambda w, q: b.rx.at[w, p, q],
                    lambda w, q: (b.xs.at[w, p, q], b.xv.at[w, p, q]), p,
                )
            if axis == "y":
                return (
                    ny, lambda d: b.py.at[wrap(y + d, ny), half], lambda w, q: b.ry.at[w, p, q],
                    lambda w, q: (b.ys.at[w, p, q], b.yv.at[w, p, q]), p,
                )
            return (
                nz, lambda d: b.pz.at[offs.index(n2 if d == -n2 else d), p], lambda w, q: b.rz.at[w, p, q],
                lambda w, q: (b.zs.at[w, p, q], b.zv.at[w, p, q]), 0 if p < nx // 2 else 1,
            )

        def count(n, w, long_way):
            return n // 2 if w == long_way else n // 2 - 1

        def hop(axis, p, w, s):
            n, sums, slot, sems, long_way = ring(axis, p)
            hops, way = count(n, w, long_way), 1 - 2 * w
            if s > hops:
                return
            chunk = sums(way * (hops - s + 1))
            if s > 1:
                arrived(slot(w, s - 2), sems(w, s - 2)[1])
                chunk[...] = (chunk[...].astype(F32) + slot(w, s - 2)[...].astype(F32)).astype(BF16)
            send(chunk, slot(w, s - 1), *sems(w, s - 1), at(axis, way))

        def gathered(axis, p):
            n, sums, slot, sems, long_way = ring(axis, p)
            total = sums(0)[...].astype(F32)
            for w in (0, 1):
                hops = count(n, w, long_way)
                if hops > 0:
                    arrived(slot(w, hops - 1), sems(w, hops - 1)[1])
                    total += slot(w, hops - 1)[...].astype(F32)
            return total.astype(BF16)

        def fold(mine, received, n):
            total = mine.astype(F32)
            for i in range(n):
                total += received[i].astype(F32)
            return total

        def to_line(axis, n, me, src, dst, ss, v):
            for d in range(1, n):
                send(src.at[wrap(me + d, n)], dst.at[d - 1], ss.at[d - 1], v, at(axis, d))

        def gather_xy():
            rows = gathered("x", 0)
            for g in range(n2):
                b.x1[:, g] = rows[g]
            for p in (1, 0):
                rows = gathered("y", p)
                for g in range(n2):
                    b.y1[:, p * n2 + g] = rows[g]
            to_line("y", ny, y, b.x1, b.x1r, b.x1s, b.x1v)
            to_line("x", nx, x, b.y1, b.y1r, b.y1s, b.y1v)

        def gather_z():
            for p in [*range(nx // 2, nx), *range(nx // 2)]:
                b.z1[p] = gathered("z", p)
            to_line("x", nx, x, b.z1, b.z1r, b.z1s, b.z1v)

        def to_places(places, src, dst, ss, v):
            for g, d in enumerate(places):
                send(src.at[g], dst.at[g], ss.at[g], v, at("z", d))

        def gather_near():
            b.xn[...] = gathered("x", 1)
            to_places(offs[n2:-1], b.xn, b.xnr, b.xns, b.xnv)

        def fold_y():
            arrived(b.y1r, b.y1v)
            rows = fold(b.y1[x], b.y1r, nx - 1).astype(BF16)
            b.far[:, :, to_y:] = rows[:n2]
            b.near[...] = rows[n2:]
            to_places(offs[n2:-1], b.near, b.near_r, b.near_s, b.near_v)

        def fold_far():
            arrived(b.x1r, b.x1v)
            b.far[:, :, :to_y] = fold(b.x1[y], b.x1r, ny - 1).astype(BF16)
            to_places(offs[:n2], b.far, b.far_r, b.far_s, b.far_v)

        def fold_z():
            arrived(b.z1r, b.z1v)
            b.z2[:, :, to_y:] = fold(b.z1[x], b.z1r, nx - 1).astype(BF16)
            total = b.xn[n2 - 1]
            if n2 > 1:
                arrived(b.xnr, b.xnv)
                total = fold(total, b.xnr, n2 - 1)
            b.z2[:, :, :to_y] = total.astype(BF16)
            to_line("y", ny, y, b.z2, b.z2r, b.z2s, b.z2v)

        def drain():
            for copy in mine:
                copy.wait_send()
            mine.clear()

        def end_far():
            total = b.near[n2 - 1].astype(F32)
            if n2 > 1:
                arrived(b.near_r, b.near_v)
                total = fold(total, b.near_r, n2 - 1)
            arrived(b.far_r, b.far_v)
            b.fin[:, to_y:to_z] = fold(total, b.far_r.at[:, :, to_y:], n2)
            b.fin[:, :to_y] = fold(b.far_r[0, :, :to_y], b.far_r.at[1:, :, :to_y], n2 - 1)

        def end_z():
            arrived(b.z2r, b.z2v)
            total = fold(b.z2[y], b.z2r, ny - 1)
            b.fin[:, :to_y] = b.fin[:, :to_y] + total[:, :to_y]
            b.fin[:, to_z:] = total[:, to_y:]

        events = []

        def add(time, f, *args):
            events.append((time, functools.partial(f, *args)))

        ready = [2.2 + 0.5 * i for i in range(nz)]
        for i in range(nz):
            add(0.0 if i < 2 else ready[i - 2] + 0.2, own_product, i)
            add(ready[i], chip_product, i)
        for w in (0, 1):
            for p in (0, 1):
                half = ready[(p + 1) * n2 - 1] + 0.1
                for s in range(1, nx // 2 + 1):
                    add(half + 9.5 * (s - 1) + 0.1, hop, "x", p, w, s)
                for s in range(1, ny // 2 + 1):
                    add(half + 5.1 * (s - 1), hop, "y", p, w, s)
            for p in range(nx):
                begin = ready[0] + 0.1 if w == (0 if p < nx // 2 else 1) else ready[min(2, nz - 1)] + 0.1
                for s in range(1, nz // 2 + 1):
                    add(begin + 4.5 * (s - 1) + 0.01 * p, hop, "z", p, w, s)
        add(26.0, gather_xy)
        add(29.0, gather_z)
        add(29.2, gather_near)
        add(30.5, fold_y)
        add(33.0, fold_far)
        add(34.0, drain)
        add(35.0, fold_z)
        add(39.0, end_far)
        add(41.0, end_z)
        for _, step in sorted(events, key=lambda e: e[0]):
            step()

        keep = ROWS // 2
        send(b.fin.at[pl.ds((1 - core) * keep, keep)], b.fin_r, b.fin_s, b.fin_v, sibling)
        out_ref[:, pl.ds(pl.multiple_of(core * cols, TILE), cols)] = b.fin[pl.ds(core * keep, keep), :]
        arrived(b.fin_r, b.fin_v)
        out_ref[:, pl.ds(pl.multiple_of((1 - core) * cols, TILE), cols)] = b.fin_r[...]
        drain()

    for c in (0, 1):
        pl.when(core == c)(functools.partial(work, c))


def shards(t, acts, key_cot, value_cot):
    tokens, width = acts.shape
    cols = key_cot.shape[1]
    held = {(None, n): r for n, r in shared_buffers(t, tokens, width, cols).items()}
    for c, share in enumerate(SHARES):
        held.update({(c, n): r for n, r in core_buffers(t, *share).items()})
    anywhere = pl.BlockSpec(memory_space=pl.ANY)
    return pl.pallas_call(
        functools.partial(kernel, t, tuple(held)),
        out_shape=jax.ShapeDtypeStruct((ROWS // 2, 2 * cols), F32),
        in_specs=[anywhere] * 3,
        out_specs=pl.BlockSpec(memory_space=pltpu.VMEM),
        scratch_shapes=list(held.values()),
        compiler_params=pltpu.CompilerParams(
            collective_id=0, has_side_effects=True, vmem_limit_bytes=56 * 2**20
        ),
        cost_estimate=pl.CostEstimate(
            flops=4 * tokens * width * cols, bytes_accessed=2 * tokens * (width + 2 * cols),
            transcendentals=0,
        ),
    )(acts, key_cot, value_cot)


def solution(mesh):
    t = Torus(mesh.shape["node"], mesh.shape["local"], 4, 8)
    placed = P(("node", "local"), None)
    return jax.shard_map(
        functools.partial(shards, t), mesh=mesh, in_specs=(placed,) * 3,
        out_specs=placed, check_vma=False,
    )
```

time: 385 us -> 69.4 us (0.18); the launches traced: 378 us -> 69.2 us
  blocking collectives: 338 us -> 0 us
  Pallas kernels: 0 us -> 67.8 us
  local copies, waits for them, and re-layouts: 24.8 us -> 1.38 us
  other arithmetic: 8.4 us -> 0 us
  matrix products: 7.41 us -> 0 us
    all_to_all x2 -> x0, blocking collectives: 338 us -> none  [the longest x1 300 us: shards(): lax.all_to_all(parts, 'local', split_axis=1, concat_axis=1, tiled=True)]
    pallas_call x0 -> x1, Pallas kernels: none -> 67.8 us  [shards(): pl.pallas_call(functools.partial(kernel, t, tuple(held)), out_shape=jax.S...]
    convert_element_type x1 -> x0, local copies, waits for them, and re-layouts: 16.6 us -> none  [local_partial(): piece.astype(jnp.bfloat16).reshape(n_node, n_local, slab, cotan.shape[1])]
    reduce_sum x2 -> x0, other arithmetic: 8.4 us -> none  [the longest x1 7.75 us: fold_group(): return jnp.sum(received.astype(jnp.float32), axis=1).astype(jnp.bfloat16)]
    dot_general x1 -> x0, matrix products: 7.41 us -> none  [local_partial(): lax.dot_general(acts, cotan, (((0,), (0,)), ((), ())), preferred_element_...]
    reshape x1 -> x0, local copies, waits for them, and re-layouts: 6.24 us -> none  [local_partial(): piece.astype(jnp.bfloat16).reshape(n_node, n_local, slab, cotan.shape[1])]
where the time goes in v4:
time: 69.4 us; the launch traced here: 69.2 us
  Pallas kernels  67.8 us (98%)
  local copies, waits for them, and re-layouts  1.38 us (2%)
    pallas_call x1, Pallas kernels, shards(): pl.pallas_call(functools.partial(kernel, t, tuple(held)), out_shape=jax.S...  67.8 us

profile of v4, /device:TPU:1, one launch (start us, length us, event | category | flops | bytes accessed | tf_op | source)
XLA Modules:
  0.0 69.2 jit_solution(12531098487573638866)
XLA Ops:
  0.0 67.8 %shard_map.37 = f32[8,1024]{1,0:T(8,128)} custom-call(bf16[256,6144]{1,0:T(8,128)(2,1)} %acts_hbm.1, bf16[256,512]{1,0:T(8,128)(2,1)} %key_hbm.1, bf16[256,512]{1,0:T(8,128)(2,1)} %value_hbm.1), custom_call_target="tpu_custom_call" | custom-call | flops 3221225472 | bytes 3670016 | tf_op jit(solution)/shard_map/pallas_call | solution.py:362
  67.8 1.4 %copy.5 = f32[8,1024]{1,0:T(8,128)} copy(f32[8,1024]{1,0:T(8,128)} %shard_map.37) | data formatting | bytes 65536

commit v5 on v4

--- a/solution.py
+++ b/solution.py
@@ -154,9 +154,14 @@
         return pl.ds(pl.multiple_of(wrap(z + offs[i], nz) * block, TILE), block)
 
     send(b.cot_give, b.cot_sib, b.pair_s.at[0], b.pair_v.at[0], sibling)
-    for i in range(nz):
+
+    def give(i):
         part = (slice(None), slice(None), cut(i))
-        send(b.acts.at[part], b.sib_acts.at[part], b.pair_s.at[1 + i], b.pair_v.at[1 + i], sibling)
+        return b.acts.at[part], b.sib_acts.at[part], b.pair_s.at[1 + i], b.pair_v.at[1 + i], sibling
+
+    early = min(3, nz)
+    for i in range(early):
+        send(*give(i))
 
     def work(c):
         mine = list(started)
@@ -315,14 +320,16 @@
             events.append((time, functools.partial(f, *args)))
 
         ready = [2.2 + 0.5 * i for i in range(nz)]
+        for i in range(early, nz):
+            add(0.1 + 0.25 * (i - early), lambda i: send(*give(i)), i)
         for i in range(nz):
-            add(0.0 if i < 2 else ready[i - 2] + 0.2, own_product, i)
+            add(0.2 * i if i < 2 else ready[i - 2] + 0.2, own_product, i)
             add(ready[i], chip_product, i)
         for w in (0, 1):
             for p in (0, 1):
                 half = ready[(p + 1) * n2 - 1] + 0.1
                 for s in range(1, nx // 2 + 1):
-                    add(half + 9.5 * (s - 1) + 0.1, hop, "x", p, w, s)
+                    add(half + (10.0 + 1.5 * p) * (s - 1) + 0.1, hop, "x", p, w, s)
                 for s in range(1, ny // 2 + 1):
                     add(half + 5.1 * (s - 1), hop, "y", p, w, s)
             for p in range(nx):
@@ -331,11 +338,11 @@
                     add(begin + 4.5 * (s - 1) + 0.01 * p, hop, "z", p, w, s)
         add(26.0, gather_xy)
         add(29.0, gather_z)
-        add(29.2, gather_near)
+        add(27.8, gather_near)
         add(30.5, fold_y)
         add(33.0, fold_far)
-        add(34.0, drain)
-        add(35.0, fold_z)
+        add(32.8, drain)
+        add(32.9, fold_z)
         add(39.0, end_far)
         add(41.0, end_z)
         for _, step in sorted(events, key=lambda e: e[0]):

time: 69.4 us -> 67 us (0.965)
  Pallas kernels: 67.8 us -> 65.4 us
    pallas_call x1, Pallas kernels: 67.8 us -> 65.4 us  [shards(): pl.pallas_call(functools.partial(kernel, t, tuple(held)), out_shape=jax.S...]
where the time goes in v5:
time: 67 us; the launch traced here: 66.8 us
  Pallas kernels  65.4 us (98%)
  local copies, waits for them, and re-layouts  1.38 us (2%)
    pallas_call x1, Pallas kernels, shards(): pl.pallas_call(functools.partial(kernel, t, tuple(held)), out_shape=jax.S...  65.4 us
    unnamed x1, local copies, waits for them, and re-layouts  1.38 us

profile of v5, /device:TPU:1, one launch (start us, length us, event | category | flops | bytes accessed | tf_op | source)
XLA Modules:
  0.0 66.8 jit_solution(9882630679097375747)
XLA Ops:
  0.0 65.4 %shard_map.37 = f32[8,1024]{1,0:T(8,128)} custom-call(bf16[256,6144]{1,0:T(8,128)(2,1)} %acts_hbm.1, bf16[256,512]{1,0:T(8,128)(2,1)} %key_hbm.1, bf16[256,512]{1,0:T(8,128)(2,1)} %value_hbm.1), custom_call_target="tpu_custom_call" | custom-call | flops 3221225472 | bytes 3670016 | tf_op jit(solution)/shard_map/pallas_call | solution.py:369
  65.5 1.4 %copy.5 = f32[8,1024]{1,0:T(8,128)} copy(f32[8,1024]{1,0:T(8,128)} %shard_map.37) | data formatting | bytes 65536
